TPU v7x, 256 devices: a whole 4x4x8 slice. The times are simulated.
256 devices in a mesh: node: 8 (over x, core), cut: 32 (over y, z).
Axes of the slice: x: 4, y: 4, z: 8, core: 2. Of those that a mesh axis runs over, the one named last changes fastest.
Arguments:
- trial_states: bfloat16 [2048, 4096], P('cut'), may hold values from -6 to 6
- cut_slopes: bfloat16 [32, 4096, 4096], P('node', 'cut'), may hold values from -0.09375 to 0.09375
- cut_intercepts: float32 [32, 4096], P('node', 'cut'), may hold values from 0 to 3
- transition: float32 [32, 32], replicated, may hold values from 0.02 to 1
Outputs:
- expected_values: float32 [32, 64, 32], P('cut', 'node')
All inputs are finite; a program needn't handle non-finite values.
Results may differ from a plain program's by a relative error of at most 0.0028.
Values may be sent and summed in bfloat16 or wider, within the bound.
A program may use at most 64 MiB of HBM per device.

v0:
```python
import jax
import jax.numpy as jnp
from jax import lax
from jax.sharding import PartitionSpec as P


def send_owners(mine):
    return lax.all_to_all(mine, "node", split_axis=0, concat_axis=1, tiled=True)


def cut_maxima(states_rows, slope_rows, offsets, node_local):
    scores = lax.dot_general(
        states_rows, slope_rows, (((1,), (1,)), ((), ())), preferred_element_type=jnp.float32
    )
    scores = scores + offsets
    return jnp.max(scores.reshape(states_rows.shape[0], node_local, -1), axis=2)


def per_device(trial_states, cut_slopes, cut_intercepts, transition):
    node_local = cut_slopes.shape[0]
    cut_local = cut_slopes.shape[1]
    width = cut_slopes.shape[2]
    trial_local = trial_states.shape[0]
    node_groups = lax.axis_size("node")
    cut_groups = lax.axis_size("cut")
    owned = trial_local // node_groups
    slope_rows = cut_slopes.reshape(node_local * cut_local, width)
    offsets = cut_intercepts.reshape(1, node_local * cut_local)
    partial_max = cut_maxima(
        lax.all_gather(trial_states, "cut", axis=0, tiled=True), slope_rows, offsets, node_local
    )
    full_max = lax.pmax(partial_max.astype(jnp.bfloat16), "cut").astype(partial_max.dtype)
    blocked = full_max.reshape(cut_groups, trial_local, node_local)
    mine = lax.dynamic_index_in_dim(blocked, lax.axis_index("cut"), 0, keepdims=False)
    owner_values = send_owners(mine)
    mixing = transition / jnp.sum(transition, axis=1, keepdims=True)
    values = jnp.dot(
        owner_values, mixing.T, precision=lax.Precision.HIGHEST, preferred_element_type=jnp.float32
    )
    return values.reshape(1, owned, values.shape[1])


def solution(mesh):
    return jax.shard_map(
        per_device,
        mesh=mesh,
        in_specs=(P("cut", None), P("node", "cut", None), P("node", "cut"), P()),
        out_specs=P("cut", "node", None),
        check_vma=False,
    )
```

profile of v0, /device:TPU:7, one launch (start us, length us, event | category | flops | bytes accessed | tf_op | source)
XLA Modules:
  0.0 323.0 jit_solution(16379834369383089056)
XLA Ops:
  6.5 0.0 all-gather.2.cloned.1.call-start
  6.5 0.7 all-gather.2.cloned.1.call-update
  7.3 145.8 %all-gather.2.cloned.1.call-done = bf16[2048,4096]{1,0:T(8,128)(2,1)} async-done(((bf16[64,4096]{1,0:T(8,128)(2,1)}), bf16[2048,4096]{1,0:T(8,128)(2,1)}) %all-gather.2.cloned.1.call-update) | async-done | bytes 16777232 | tf_op jit(solution)/shard_map/all_gather | solution.py:30
  153.1 0.0 copy-start
  153.1 13.7 %bitcast_reduce_fusion = bf16[2048,4]{0,1:T(4,128)(2,1)S(1)} fusion(f32[512]{0:T(512)} %bitcast.18, bf16[2048,4096]{1,0:T(8,128)(2,1)} %all-gather.2.cloned.1.call-done, bf16[512,4096]{1,0:T(8,128)(2,1)} %bitcast.17), kind=kOutput, calls=%fused_computation | convolution fusion | flops 8592023552 | bytes 20989952 | tf_op jit(solution)/shard_map/dot_general | solution.py:12
  166.8 0.1 reshape.24
  166.9 111.9 %pmax.7 = bf16[32,64,4]{1,0,2:T(8,128)(2,1)S(1)} all-reduce(bf16[32,64,4]{1,0,2:T(8,128)(2,1)S(1)} %reshape.24), channel_id=1, replica_groups=mesh['node'=8,'cut'=32] {'cut'}, use_global_device_ids=true, to_apply=%region_1.0 | all-reduce | flops 8192 | bytes 32768 | tf_op jit(solution)/shard_map/pmax | solution.py:32
  278.8 0.1 all_to_all.14
  278.8 0.6 copy.7
  279.4 33.0 %all-to-all-start = ((f32[8,8,4]{1,2,0:T(4,128)}), f32[8,8,4]{1,2,0:T(4,128)S(1)}, u32[]{:S(2)}, u32[]{:S(2)}) async-start(f32[8,8,4]{1,2,0:T(4,128)} %copy.7), calls=%async_computation | async-start | bytes 32768 | tf_op jit(solution)/shard_map/all_to_all | solution.py:8
  312.4 0.0 copy-done
  312.4 0.1 reduce_sum.9
  312.5 2.8 all-to-all-done
  315.4 0.8 convolution_bitcast_fusion
  (1 shorter events, 0.0 us)
Async XLA Ops:
  6.5 146.6 %all-gather.2.cloned.1.call-start = ((), (), s32[]{:S(2)}) async-start(), calls=%async_computation.1 | async-start | bytes 17301504 | tf_op jit(solution)/shard_map/all_gather | solution.py:30
  153.1 159.3 %copy-start = (f32[32,32]{1,0:T(8,128)S(1)}, f32[32,32]{1,0:T(8,128)}, u32[]{:S(2)}) copy-start(f32[32,32]{1,0:T(8,128)} %param.7) | copy-start | bytes 12292
  279.4 35.9 %all-to-all-start = ((f32[8,8,4]{1,2,0:T(4,128)}), f32[8,8,4]{1,2,0:T(4,128)S(1)}, u32[]{:S(2)}, u32[]{:S(2)}) async-start(f32[8,8,4]{1,2,0:T(4,128)} %copy.7), calls=%async_computation | async-start | bytes 32768 | tf_op jit(solution)/shard_map/all_to_all | solution.py:8
Sparse Core Ops, SparseCore 0:
  10.0 143.1 all-gather.1
where the time goes:
time: 326 us; the launch traced here: 323 us
  waiting for transfers between devices  149 us (46%)
  blocking collectives  112 us (34%)
  starting transfers between devices  33 us (10%)
  matrix products  14.5 us (4%)
  between operations  13.4 us (4%)
    all_gather x1, waiting for transfers between devices, per_device(): lax.all_gather(trial_states, 'cut', axis=0, tiled=True)  146 us
    pmax x1, blocking collectives, per_device(): lax.pmax(partial_max.astype(jnp.bfloat16), 'cut').astype(partial_max.dtype)  112 us
    all_to_all x1, starting transfers between devices, send_owners(): return lax.all_to_all(mine, 'node', split_axis=0, concat_axis=1, tiled=True)  33 us
    dot_general x1, matrix products, cut_maxima(): lax.dot_general(states_rows, slope_rows, (((1,), (1,)), ((), ())), prefer...  13.7 us
  transfers between devices with their start and end apart: 2, of which 2 were waited for; matrix products, arithmetic and copies ran while one was open for 0% of the time, Pallas kernels for 0%

commit v1 on v0

v1 whole, which is shorter than its diff:
```python
import functools

import jax
import jax.numpy as jnp
from jax import lax
from jax.experimental import pallas as pl
from jax.experimental.pallas import tpu as pltpu
from jax.sharding import PartitionSpec as P

MESH = pl.DeviceIdType.MESH

NY, NZ, NX = 4, 8, 4

FETCH = 2816

PZ, MZ, PY, MY = (0, 1), (0, -1), (1, 0), (-1, 0)
LINKS = (PZ, MZ, PY, MY)

CROSS = {
    PZ: [(0, 1), (0, 2), (0, 3), (2, 1), (0, 4), (2, 2), (2, 3), (1, 4)],
    MZ: [(0, -1), (0, -2), (0, -3), (2, -1), (2, -2), (2, -3), (2, 4)],
    PY: [(1, 0), (2, 0), (1, 1), (1, -1), (1, 2), (1, -2), (1, 3), (1, -3)],
    MY: [(-1, 0), (-1, 1), (-1, -1), (-1, 2), (-1, -2), (-1, 3), (-1, -3), (-1, 4)],
}
HALVES = (0, 1)


def wrap(o):
    return (o[0] % NY, o[1] % NZ)


def plan(window, span, delay):
    todo = {d: [(wrap(o), h) for o in order for h in HALVES] for d, order in CROSS.items()}
    here = {((0, 0), h) for h in HALVES}
    free = dict.fromkeys(LINKS, 0.0)
    flying = dict.fromkeys(LINKS, 0)
    arrivals = []

    def issue(now):
        sends = []
        for d in LINKS:
            for o, h in list(todo[d]):
                source = wrap((o[0] - d[0], o[1] - d[1]))
                if flying[d] < window and (source, h) in here:
                    todo[d].remove((o, h))
                    flying[d] += 1
                    free[d] = max(free[d], now) + span
                    arrivals.append((free[d] + delay, len(arrivals), d, o, h))
                    sends.append((source, h, d))
        return sends

    first = issue(0.0)
    turns = []
    while len(turns) < len(arrivals):
        now, _, d, o, h = sorted(arrivals)[len(turns)]
        here.add((o, h))
        flying[d] -= 1
        turns.append((o, h, issue(now)))
    return first, turns


FIRST, TURNS = plan(window=3, span=1.8, delay=2.5)
PLACE = {(0, 0): 0}
for o, h, _ in TURNS:
    if (o, 1 - h) in [t[:2] for t in TURNS[:TURNS.index((o, h, _))]]:
        PLACE[o] = len(PLACE)
ARRIVALS = sorted(PLACE, key=PLACE.get)
PIECES = 8
NEED = [1 + max(i for i, t in enumerate(TURNS) if PLACE[t[0]] < 8 * g + 8) for g in range(4)]
STEPS = 3 * PIECES


def handled(step):
    group, which = step // PIECES, step % PIECES
    if step < 0:
        return 0
    return NEED[group] + (NEED[min(group + 1, 3)] - NEED[group]) * which // PIECES


def kernel(
    trial_ref, slope_ref, offset_ref, trans_ref, out_ref,
    gath, slopes, offset, weights, icol, sums, part, got, nodev, vals,
    local_sem, swap_send, swap_recv, yz_send, yz_recv, x_send, x_recv, a_send, a_recv, b_send, b_recv,
):
    node = lax.axis_index("node")
    cut = lax.axis_index("cut")
    x, core = node // 2, node % 2
    y, z = cut // NZ, cut % NZ
    odd = x % 2
    sibling = x * 2 + 1 - core
    share = 1 - core
    width = trial_ref.shape[1]
    own_rows = slope_ref.shape[0]
    rows = gath.shape[1]
    hrows = rows // 2
    extra = width - FETCH
    fetch_at = pl.multiple_of(odd * extra, 128)
    mine_at = pl.multiple_of(odd * FETCH, 128)
    other_at = pl.multiple_of((1 - odd) * FETCH, 128)
    beside = {d: ((y + d[0] + NY) % NY) * NZ + (z + d[1] + NZ) % NZ for d in LINKS}

    def yz_copy(o, h, d):
        oc = wrap((o[0] + d[0], o[1] + d[1]))
        piece = (pl.ds(h * hrows, hrows), pl.ds(fetch_at, FETCH))
        source = gath.at[PLACE[o], *piece]
        if o == (0, 0):
            source = trial_ref.at[pl.ds(share * rows + h * hrows, hrows), pl.ds(fetch_at, FETCH)]
        return pltpu.make_async_remote_copy(
            src_ref=source, dst_ref=gath.at[PLACE[oc], *piece],
            send_sem=yz_send, recv_sem=yz_recv.at[PLACE[oc] - 1, h],
            device_id=(node, beside[d]), device_id_type=MESH,
        )

    def yz_arrived(o, h):
        ref = gath.at[PLACE[o], pl.ds(h * hrows, hrows), pl.ds(fetch_at, FETCH)]
        pltpu.make_async_copy(ref, ref, yz_recv.at[PLACE[o] - 1, h]).wait()

    def x_copy(o, h):
        ref = gath.at[PLACE[o], pl.ds(h * hrows, hrows), pl.ds(mine_at, extra)]
        to = ((x + (1 if h == 0 else NX - 1)) % NX) * 2 + core
        return pltpu.make_async_remote_copy(
            src_ref=ref, dst_ref=ref, send_sem=x_send, recv_sem=x_recv.at[PLACE[o] // 8],
            device_id=(to, cut), device_id_type=MESH,
        )

    def x_arrived(group):
        low = max(8 * group, 1)
        ref = gath.at[pl.ds(low, 8 * group + 8 - low), :, pl.ds(other_at, extra)]
        pltpu.make_async_copy(ref, ref, x_recv.at[group]).wait()

    def product(group, m, at, lanes):
        span = pl.ds(at, lanes)
        states = gath[pl.ds(8 * group, 8), :, span].reshape(8 * rows, lanes)
        return lax.dot_general(
            slopes[pl.ds(m * 256, 256), span], states, (((1,), (1,)), ((), ())),
            preferred_element_type=jnp.float32,
        )

    def compute(piece):
        group = lax.div(piece, PIECES)
        m = lax.rem(piece, PIECES // 2)

        @pl.when(lax.rem(piece, PIECES) < PIECES // 2)
        def _():
            sums[m] = product(group, m, fetch_at, FETCH)

        @pl.when(lax.rem(piece, PIECES) >= PIECES // 2)
        def _():
            add = icol[m]
            total = sums[m] + product(group, m, other_at, extra) + jnp.concatenate([add, add], axis=1)
            best = jnp.max(total.reshape(2, 128, 8 * rows), axis=1)
            part[2 * group, m] = best[:, 0:128]
            part[2 * group + 1, m] = best[:, 128:256]

    def finish():
        def whole(at, lanes):
            span = pl.ds(at, lanes)
            states = gath[pl.ds(24, 8), :, span].reshape(8 * rows, lanes)
            return lax.dot_general(
                slopes[:, span], states, (((1,), (1,)), ((), ())), preferred_element_type=jnp.float32
            )

        sums[...] = whole(fetch_at, FETCH).reshape(sums.shape)
        x_arrived(3)
        rest = whole(other_at, extra).reshape(sums.shape)
        for m in range(4):
            add = icol[m]
            total = sums[m] + rest[m] + jnp.concatenate([add, add], axis=1)
            best = jnp.max(total.reshape(2, 128, 8 * rows), axis=1)
            part[6, m] = best[:, 0:128]
            part[7, m] = best[:, 128:256]

    def tell(group):
        for i in range(max(8 * group, 1), 8 * group + 8):
            o = ARRIVALS[i]
            owner = ((y - o[0] + NY) % NY) * NZ + (z - o[1] + NZ) % NZ
            pltpu.make_async_remote_copy(
                src_ref=part.at[i // 4], dst_ref=got.at[i - 1], send_sem=a_send, recv_sem=a_recv,
                device_id=(node, owner), device_id_type=MESH,
            ).start()

    own = pltpu.make_async_copy(trial_ref.at[pl.ds(share * rows, rows)], gath.at[0], local_sem.at[0])
    load = pltpu.make_async_copy(slope_ref, slopes.at[pl.ds(core * own_rows, own_rows)], local_sem.at[1])
    load_offset = pltpu.make_async_copy(offset_ref, offset.at[core], local_sem.at[2])
    load_trans = pltpu.make_async_copy(trans_ref, weights, local_sem.at[3])
    swap = pltpu.make_async_remote_copy(
        src_ref=slope_ref, dst_ref=slopes.at[pl.ds(core * own_rows, own_rows)],
        send_sem=swap_send.at[0], recv_sem=swap_recv.at[0],
        device_id=(sibling, cut), device_id_type=MESH,
    )
    swap_offset = pltpu.make_async_remote_copy(
        src_ref=offset_ref, dst_ref=offset.at[core],
        send_sem=swap_send.at[1], recv_sem=swap_recv.at[1],
        device_id=(sibling, cut), device_id_type=MESH,
    )
    barrier = pltpu.get_barrier_semaphore()
    for d in LINKS:
        pl.semaphore_signal(barrier, inc=1, device_id=(node, beside[d]), device_id_type=MESH)
    for j in range(1, 8):
        pl.semaphore_signal(barrier, inc=1, device_id=((node + j) % 8, cut), device_id_type=MESH)
    own.start()
    load_offset.start()
    load_trans.start()
    pl.semaphore_wait(barrier, 11)

    for o, h, d in FIRST:
        yz_copy(o, h, d).start()
    swap_offset.start()
    swap.start()
    load.start()
    load_offset.wait()
    swap_offset.wait()
    for c in range(2):
        for n in range(4):
            line = jnp.broadcast_to(offset[c, n:n + 1, :], (128, 128))
            icol[2 * c + n // 2, pl.ds(n % 2 * 128, 128), :] = line.T

    def talk(k):
        for o, h, sends in TURNS[handled(k - 1):handled(k)]:
            yz_arrived(o, h)
            for send in sends:
                yz_copy(*send).start()
            x_copy(o, h).start()
        if k == 0:
            own.wait()
            load.wait()
            swap.wait()
        if k % PIECES == 0 and k > 0:
            tell(k // PIECES - 1)
        if k % PIECES == PIECES // 2:
            x_arrived(k // PIECES)

    def choose(step, low, high):
        if high - low == 1:
            talk(low)
            return
        mid = (low + high) // 2

        @pl.when(step < mid)
        def _():
            choose(step, low, mid)

        @pl.when(step >= mid)
        def _():
            choose(step, mid, high)

    def turn(step, carry):
        choose(step, 0, STEPS)
        compute(step)
        return carry

    lax.fori_loop(0, STEPS, turn, 0)
    talk(STEPS)
    finish()
    tell(3)

    for at, lanes, sem in ((fetch_at, FETCH, yz_send), (mine_at, extra, x_send)):
        ref = gath.at[pl.ds(0, len(ARRIVALS) - 1), :, pl.ds(at, lanes)]
        pltpu.make_async_copy(ref, ref, sem).wait()
    pltpu.make_async_copy(got, got, a_recv).wait()
    pltpu.make_async_copy(got, got, a_send).wait()
    best = None
    for q in range(4):
        tiles = [got[i - 1] for i in range(q, len(ARRIVALS), 4) if i > 0]
        if q == 0:
            tiles.append(part[0])
        top = functools.reduce(jnp.maximum, tiles)[:, :, q * rows:(q + 1) * rows]
        best = top if best is None else jnp.maximum(best, top)
    nodev[node, :, :, 0:rows] = best
    for j in range(4):
        to = 4 * share + j

        @pl.when(to != node)
        def _():
            pltpu.make_async_remote_copy(
                src_ref=nodev.at[node], dst_ref=nodev.at[node], send_sem=b_send, recv_sem=b_recv,
                device_id=(to, cut), device_id_type=MESH,
            ).start()

    load_trans.wait()
    trans = weights[...]
    mixing = trans / jnp.sum(trans, axis=1, keepdims=True)
    holder = 1 - node // 4
    keeps = holder == core

    @pl.when(keeps)
    def _():
        ref = nodev.at[pl.ds(0, 3)]
        pltpu.make_async_copy(ref, ref, b_recv).wait()
        pltpu.make_async_copy(ref, ref, b_send).wait()

    @pl.when(jnp.logical_not(keeps))
    def _():
        ref = nodev.at[pl.ds(0, 4)]
        pltpu.make_async_copy(ref, ref, b_recv).wait()
        pltpu.make_async_copy(ref, ref, b_send).wait()

    known = jnp.concatenate(
        [nodev[2 * i + holder, m, :, 0:rows] for i in range(NX) for m in range(4)], axis=0
    )
    vals[...] = lax.dot_general(
        known.T, mixing, (((1,), (1,)), ((), ())),
        precision=lax.Precision.HIGHEST, preferred_element_type=jnp.float32,
    )
    out_ref[0] = vals[pl.ds(pl.multiple_of((node % 4) * 8, 8), 8), :]


def per_device(trial_states, cut_slopes, cut_intercepts, transition):
    node_local, cut_local, width = cut_slopes.shape
    rows = trial_states.shape[0]
    nodes = transition.shape[0]
    slope_rows = cut_slopes.reshape(node_local * cut_local, width)
    count = len(ARRIVALS)
    sems = pltpu.SemaphoreType.DMA
    return pl.pallas_call(
        kernel,
        out_shape=jax.ShapeDtypeStruct((1, rows // 8, nodes), jnp.float32),
        in_specs=[pl.BlockSpec(memory_space=pltpu.HBM)] * 4,
        out_specs=pl.BlockSpec(memory_space=pltpu.VMEM),
        scratch_shapes=[
            pltpu.VMEM((count, rows // 2, width), jnp.bfloat16),
            pltpu.VMEM((2 * node_local * cut_local, width), jnp.bfloat16),
            pltpu.VMEM((2, node_local, cut_local), jnp.float32),
            pltpu.VMEM(transition.shape, jnp.float32),
            pltpu.VMEM((4, 2 * cut_local, 128), jnp.float32),
            pltpu.VMEM((4, 2 * cut_local, 4 * rows), jnp.float32),
            pltpu.VMEM((count // 4, 4, 2, 128), jnp.float32),
            pltpu.VMEM((count - 1, 4, 2, 128), jnp.float32),
            pltpu.VMEM((8, 4, 2, 128), jnp.float32),
            pltpu.VMEM((rows // 2, nodes), jnp.float32),
            sems((4,)),
            sems((2,)),
            sems((2,)),
            sems(()),
            sems((count - 1, 2)),
            sems(()),
            sems((count // 8,)),
            sems(()),
            sems(()),
            sems(()),
            sems(()),
        ],
        compiler_params=pltpu.CompilerParams(
            collective_id=0, has_side_effects=True, vmem_limit_bytes=40 * 1024 * 1024
        ),
        cost_estimate=pl.CostEstimate(
            flops=2 * 512 * 2048 * 4096, bytes_accessed=5 * 1024 * 1024, transcendentals=0
        ),
    )(*[
        pltpu.with_memory_space_constraint(v, pltpu.HBM)
        for v in (trial_states, slope_rows, cut_intercepts, transition)
    ])


def solution(mesh):
    return jax.shard_map(
        per_device,
        mesh=mesh,
        in_specs=(P("cut", None), P("node", "cut", None), P("node", "cut"), P()),
        out_specs=P("cut", "node", None),
        check_vma=False,
    )
```

time: 326 us -> 58.4 us (0.18)
  waiting for transfers between devices: 149 us -> 0 us
  blocking collectives: 112 us -> 0 us
  Pallas kernels: 0 us -> 57.7 us
  starting transfers between devices: 33 us -> 0 us
  matrix products: 14.5 us -> 0 us
  between operations: 13.4 us -> 0.01 us
    all_gather x1 -> x0, waiting for transfers between devices: 146 us -> none  [per_device(): lax.all_gather(trial_states, 'cut', axis=0, tiled=True)]
    pmax x1 -> x0, blocking collectives: 112 us -> none  [per_device(): lax.pmax(partial_max.astype(jnp.bfloat16), 'cut').astype(partial_max.dtype)]
    pallas_call x0 -> x1, Pallas kernels: none -> 57.7 us  [per_device(): pl.pallas_call(kernel, out_shape=jax.ShapeDtypeStruct((1, rows // 8, node...]
    all_to_all x1 -> x0, starting transfers between devices: 33 us -> none  [send_owners(): return lax.all_to_all(mine, 'node', split_axis=0, concat_axis=1, tiled=True)]
    dot_general x2 -> x0, matrix products: 14.5 us -> none  [the longest x1 13.7 us: cut_maxima(): lax.dot_general(states_rows, slope_rows, (((1,), (1,)), ((), ())), prefer...]
  transfers between devices with their start and end apart: 2 -> 0, of which waited for: 2 -> 0; matrix products, arithmetic and copies ran while one was open for 0% -> 0% of each run, Pallas kernels for 0% -> 0%
where the time goes in v1:
time: 58.4 us; the launch traced here: 58.3 us
  Pallas kernels  57.7 us (99%)
  local copies, waits for them, and re-layouts  0.6 us (1%)
    pallas_call x1, Pallas kernels, per_device(): pl.pallas_call(kernel, out_shape=jax.ShapeDtypeStruct((1, rows // 8, node...  57.7 us

profile of v1, /device:TPU:7, one launch (start us, length us, event | category | flops | bytes accessed | tf_op | source)
XLA Modules:
  0.0 58.3 jit_solution(6413832751877413841)
XLA Ops:
  0.0 57.7 %shard_map.46 = f32[1,8,32]{2,1,0:T(8,128)S(1)} custom-call(bf16[64,4096]{1,0:T(8,128)(2,1)} %trial_ref.1, bf16[512,4096]{1,0:T(8,128)(2,1)} %bitcast.1, f32[4,128]{1,0:T(4,128)} %offset_ref.1, f32[32,32]{1,0:T(8,128)} %trans_ref.1), custom_call_target="tpu_custom_call" | custom-call | flops 8589934592 | bytes 5242880 | tf_op jit(solution)/shard_map/pallas_call | solution.py:315
  57.7 0.6 %copy.6 = f32[1,8,32]{2,1,0:T(8,128)} copy(f32[1,8,32]{2,1,0:T(8,128)S(1)} %shard_map.46) | data formatting | bytes 2048

commit v2 on v1

--- a/solution.py
+++ b/solution.py
@@ -11,7 +11,8 @@
 
 NY, NZ, NX = 4, 8, 4
 
-FETCH = 2816
+TILE, OVER, MIDDLE = 128, 10, 12
+FETCH = OVER + MIDDLE
 
 PZ, MZ, PY, MY = (0, 1), (0, -1), (1, 0), (-1, 0)
 LINKS = (PZ, MZ, PY, MY)
@@ -22,7 +23,7 @@
     PY: [(1, 0), (2, 0), (1, 1), (1, -1), (1, 2), (1, -2), (1, 3), (1, -3)],
     MY: [(-1, 0), (-1, 1), (-1, -1), (-1, 2), (-1, -2), (-1, 3), (-1, -3), (-1, 4)],
 }
-HALVES = (0, 1)
+PARTS = (0, 1)
 
 
 def wrap(o):
@@ -30,8 +31,8 @@
 
 
 def plan(window, span, delay):
-    todo = {d: [(wrap(o), h) for o in order for h in HALVES] for d, order in CROSS.items()}
-    here = {((0, 0), h) for h in HALVES}
+    todo = {d: [(wrap(o), h) for o in order for h in PARTS] for d, order in CROSS.items()}
+    here = {((0, 0), h) for h in PARTS}
     free = dict.fromkeys(LINKS, 0.0)
     flying = dict.fromkeys(LINKS, 0)
     arrivals = []
@@ -89,35 +90,32 @@
     odd = x % 2
     sibling = x * 2 + 1 - core
     share = 1 - core
-    width = trial_ref.shape[1]
+    tiles = gath.shape[1]
     own_rows = slope_ref.shape[0]
-    rows = gath.shape[1]
-    hrows = rows // 2
-    extra = width - FETCH
-    fetch_at = pl.multiple_of(odd * extra, 128)
-    mine_at = pl.multiple_of(odd * FETCH, 128)
-    other_at = pl.multiple_of((1 - odd) * FETCH, 128)
+    rows = gath.shape[2]
+    fetch_at = odd * OVER
+    mine_at = odd * FETCH
+    other_at = (1 - odd) * FETCH
     beside = {d: ((y + d[0] + NY) % NY) * NZ + (z + d[1] + NZ) % NZ for d in LINKS}
+
+    def part_of(o, h):
+        return gath.at[PLACE[o], pl.ds(mine_at, OVER) if h == 0 else pl.ds(OVER, MIDDLE)]
 
     def yz_copy(o, h, d):
         oc = wrap((o[0] + d[0], o[1] + d[1]))
-        piece = (pl.ds(h * hrows, hrows), pl.ds(fetch_at, FETCH))
-        source = gath.at[PLACE[o], *piece]
-        if o == (0, 0):
-            source = trial_ref.at[pl.ds(share * rows + h * hrows, hrows), pl.ds(fetch_at, FETCH)]
         return pltpu.make_async_remote_copy(
-            src_ref=source, dst_ref=gath.at[PLACE[oc], *piece],
+            src_ref=part_of(o, h), dst_ref=part_of(oc, h),
             send_sem=yz_send, recv_sem=yz_recv.at[PLACE[oc] - 1, h],
             device_id=(node, beside[d]), device_id_type=MESH,
         )
 
     def yz_arrived(o, h):
-        ref = gath.at[PLACE[o], pl.ds(h * hrows, hrows), pl.ds(fetch_at, FETCH)]
+        ref = part_of(o, h)
         pltpu.make_async_copy(ref, ref, yz_recv.at[PLACE[o] - 1, h]).wait()
 
-    def x_copy(o, h):
-        ref = gath.at[PLACE[o], pl.ds(h * hrows, hrows), pl.ds(mine_at, extra)]
-        to = ((x + (1 if h == 0 else NX - 1)) % NX) * 2 + core
+    def x_copy(o, way):
+        ref = gath.at[PLACE[o], pl.ds(mine_at + way * (OVER // 2), OVER // 2)]
+        to = ((x + (1 if way == 0 else NX - 1)) % NX) * 2 + core
         return pltpu.make_async_remote_copy(
             src_ref=ref, dst_ref=ref, send_sem=x_send, recv_sem=x_recv.at[PLACE[o] // 8],
             device_id=(to, cut), device_id_type=MESH,
@@ -125,14 +123,14 @@
 
     def x_arrived(group):
         low = max(8 * group, 1)
-        ref = gath.at[pl.ds(low, 8 * group + 8 - low), :, pl.ds(other_at, extra)]
+        ref = gath.at[pl.ds(low, 8 * group + 8 - low), pl.ds(other_at, OVER)]
         pltpu.make_async_copy(ref, ref, x_recv.at[group]).wait()
 
-    def product(group, m, at, lanes):
-        span = pl.ds(at, lanes)
-        states = gath[pl.ds(8 * group, 8), :, span].reshape(8 * rows, lanes)
+    def product(group, at, count, low, size):
+        left = [slopes[at + k, pl.ds(low, size), :] for k in range(count)]
+        right = [gath[pl.ds(8 * group, 8), at + k].reshape(8 * rows, TILE) for k in range(count)]
         return lax.dot_general(
-            slopes[pl.ds(m * 256, 256), span], states, (((1,), (1,)), ((), ())),
+            jnp.concatenate(left, axis=1), jnp.concatenate(right, axis=1), (((1,), (1,)), ((), ())),
             preferred_element_type=jnp.float32,
         )
 
@@ -142,27 +140,20 @@
 
         @pl.when(lax.rem(piece, PIECES) < PIECES // 2)
         def _():
-            sums[m] = product(group, m, fetch_at, FETCH)
+            sums[m] = product(group, fetch_at, FETCH, m * 256, 256)
 
         @pl.when(lax.rem(piece, PIECES) >= PIECES // 2)
         def _():
             add = icol[m]
-            total = sums[m] + product(group, m, other_at, extra) + jnp.concatenate([add, add], axis=1)
+            total = sums[m] + product(group, other_at, OVER, m * 256, 256) + jnp.concatenate([add, add], axis=1)
             best = jnp.max(total.reshape(2, 128, 8 * rows), axis=1)
             part[2 * group, m] = best[:, 0:128]
             part[2 * group + 1, m] = best[:, 128:256]
 
     def finish():
-        def whole(at, lanes):
-            span = pl.ds(at, lanes)
-            states = gath[pl.ds(24, 8), :, span].reshape(8 * rows, lanes)
-            return lax.dot_general(
-                slopes[:, span], states, (((1,), (1,)), ((), ())), preferred_element_type=jnp.float32
-            )
-
-        sums[...] = whole(fetch_at, FETCH).reshape(sums.shape)
+        sums[...] = product(3, fetch_at, FETCH, 0, 2 * own_rows).reshape(sums.shape)
         x_arrived(3)
-        rest = whole(other_at, extra).reshape(sums.shape)
+        rest = product(3, other_at, OVER, 0, 2 * own_rows).reshape(sums.shape)
         for m in range(4):
             add = icol[m]
             total = sums[m] + rest[m] + jnp.concatenate([add, add], axis=1)
@@ -179,13 +170,24 @@
                 device_id=(node, owner), device_id_type=MESH,
             ).start()
 
-    own = pltpu.make_async_copy(trial_ref.at[pl.ds(share * rows, rows)], gath.at[0], local_sem.at[0])
-    load = pltpu.make_async_copy(slope_ref, slopes.at[pl.ds(core * own_rows, own_rows)], local_sem.at[1])
+    def column(k):
+        return pl.ds(pl.multiple_of(k * TILE, TILE), TILE)
+
+    def own(k):
+        return pltpu.make_async_copy(
+            trial_ref.at[pl.ds(share * rows, rows), column(k)], gath.at[0, k], local_sem.at[0]
+        )
+
+    def load(k):
+        return pltpu.make_async_copy(
+            slope_ref.at[:, column(k)], slopes.at[k, pl.ds(core * own_rows, own_rows)], local_sem.at[1]
+        )
+
+    loaded = slopes.at[:, pl.ds(core * own_rows, own_rows)]
     load_offset = pltpu.make_async_copy(offset_ref, offset.at[core], local_sem.at[2])
     load_trans = pltpu.make_async_copy(trans_ref, weights, local_sem.at[3])
     swap = pltpu.make_async_remote_copy(
-        src_ref=slope_ref, dst_ref=slopes.at[pl.ds(core * own_rows, own_rows)],
-        send_sem=swap_send.at[0], recv_sem=swap_recv.at[0],
+        src_ref=loaded, dst_ref=loaded, send_sem=swap_send.at[0], recv_sem=swap_recv.at[0],
         device_id=(sibling, cut), device_id_type=MESH,
     )
     swap_offset = pltpu.make_async_remote_copy(
@@ -198,16 +200,18 @@
         pl.semaphore_signal(barrier, inc=1, device_id=(node, beside[d]), device_id_type=MESH)
     for j in range(1, 8):
         pl.semaphore_signal(barrier, inc=1, device_id=((node + j) % 8, cut), device_id_type=MESH)
-    own.start()
+    for k in range(tiles):
+        own(k).start()
     load_offset.start()
     load_trans.start()
     pl.semaphore_wait(barrier, 11)
+    pltpu.make_async_copy(gath.at[0], gath.at[0], local_sem.at[0]).wait()
 
     for o, h, d in FIRST:
         yz_copy(o, h, d).start()
     swap_offset.start()
-    swap.start()
-    load.start()
+    for k in range(tiles):
+        load(k).start()
     load_offset.wait()
     swap_offset.wait()
     for c in range(2):
@@ -215,15 +219,18 @@
             line = jnp.broadcast_to(offset[c, n:n + 1, :], (128, 128))
             icol[2 * c + n // 2, pl.ds(n % 2 * 128, 128), :] = line.T
 
+    pltpu.make_async_copy(loaded, loaded, local_sem.at[1]).wait()
+    swap.start()
+
     def talk(k):
         for o, h, sends in TURNS[handled(k - 1):handled(k)]:
             yz_arrived(o, h)
             for send in sends:
                 yz_copy(*send).start()
-            x_copy(o, h).start()
+            if h == 0:
+                x_copy(o, 0).start()
+                x_copy(o, 1).start()
         if k == 0:
-            own.wait()
-            load.wait()
             swap.wait()
         if k % PIECES == 0 and k > 0:
             tell(k // PIECES - 1)
@@ -254,8 +261,8 @@
     finish()
     tell(3)
 
-    for at, lanes, sem in ((fetch_at, FETCH, yz_send), (mine_at, extra, x_send)):
-        ref = gath.at[pl.ds(0, len(ARRIVALS) - 1), :, pl.ds(at, lanes)]
+    for count, sem in ((FETCH, yz_send), (OVER, x_send)):
+        ref = gath.at[pl.ds(0, len(ARRIVALS) - 1), pl.ds(0, count)]
         pltpu.make_async_copy(ref, ref, sem).wait()
     pltpu.make_async_copy(got, got, a_recv).wait()
     pltpu.make_async_copy(got, got, a_send).wait()
@@ -318,8 +325,8 @@
         in_specs=[pl.BlockSpec(memory_space=pltpu.HBM)] * 4,
         out_specs=pl.BlockSpec(memory_space=pltpu.VMEM),
         scratch_shapes=[
-            pltpu.VMEM((count, rows // 2, width), jnp.bfloat16),
-            pltpu.VMEM((2 * node_local * cut_local, width), jnp.bfloat16),
+            pltpu.VMEM((count, width // TILE, rows // 2, TILE), jnp.bfloat16),
+            pltpu.VMEM((width // TILE, 2 * node_local * cut_local, TILE), jnp.bfloat16),
             pltpu.VMEM((2, node_local, cut_local), jnp.float32),
             pltpu.VMEM(transition.shape, jnp.float32),
             pltpu.VMEM((4, 2 * cut_local, 128), jnp.float32),

time: 58.4 us -> 56.9 us (0.974)
  Pallas kernels: 57.7 us -> 56.3 us
    pallas_call x1, Pallas kernels: 57.7 us -> 56.3 us  [per_device(): pl.pallas_call(kernel, out_shape=jax.ShapeDtypeStruct((1, rows // 8, node...]
where the time goes in v2:
time: 56.9 us
  Pallas kernels  56.3 us (99%)
  local copies, waits for them, and re-layouts  0.6 us (1%)
    pallas_call x1, Pallas kernels, per_device(): pl.pallas_call(kernel, out_shape=jax.ShapeDtypeStruct((1, rows // 8, node...  56.3 us

profile of v2, /device:TPU:7, one launch (start us, length us, event | category | flops | bytes accessed | tf_op | source)
XLA Modules:
  0.0 56.9 jit_solution(3718425696065535825)
XLA Ops:
  0.0 56.3 %shard_map.46 = f32[1,8,32]{2,1,0:T(8,128)S(1)} custom-call(bf16[64,4096]{1,0:T(8,128)(2,1)} %trial_ref.1, bf16[512,4096]{1,0:T(8,128)(2,1)} %bitcast.1, f32[4,128]{1,0:T(4,128)} %offset_ref.1, f32[32,32]{1,0:T(8,128)} %trans_ref.1), custom_call_target="tpu_custom_call" | custom-call | flops 8589934592 | bytes 5242880 | tf_op jit(solution)/shard_map/pallas_call | solution.py:322
  56.3 0.6 %copy.6 = f32[1,8,32]{2,1,0:T(8,128)} copy(f32[1,8,32]{2,1,0:T(8,128)S(1)} %shard_map.46) | data formatting | bytes 2048

commit v3 on v2

--- a/solution.py
+++ b/solution.py
@@ -66,9 +66,9 @@
     if (o, 1 - h) in [t[:2] for t in TURNS[:TURNS.index((o, h, _))]]:
         PLACE[o] = len(PLACE)
 ARRIVALS = sorted(PLACE, key=PLACE.get)
-PIECES = 8
+PIECES = 4
 NEED = [1 + max(i for i, t in enumerate(TURNS) if PLACE[t[0]] < 8 * g + 8) for g in range(4)]
-STEPS = 3 * PIECES
+STEPS = 4 * PIECES
 
 
 def handled(step):
@@ -80,7 +80,7 @@
 
 def kernel(
     trial_ref, slope_ref, offset_ref, trans_ref, out_ref,
-    gath, slopes, offset, weights, icol, sums, part, got, nodev, vals,
+    gath, slopes, offset, weights, sums, part, got, nodev, vals,
     local_sem, swap_send, swap_recv, yz_send, yz_recv, x_send, x_recv, a_send, a_recv, b_send, b_recv,
 ):
     node = lax.axis_index("node")
@@ -126,9 +126,10 @@
         ref = gath.at[pl.ds(low, 8 * group + 8 - low), pl.ds(other_at, OVER)]
         pltpu.make_async_copy(ref, ref, x_recv.at[group]).wait()
 
-    def product(group, at, count, low, size):
-        left = [slopes[at + k, pl.ds(low, size), :] for k in range(count)]
-        right = [gath[pl.ds(8 * group, 8), at + k].reshape(8 * rows, TILE) for k in range(count)]
+    def product(group, at, count, owner):
+        low = owner * own_rows
+        left = [gath[pl.ds(8 * group, 8), at + k].reshape(8 * rows, TILE) for k in range(count)]
+        right = [slopes[at + k, pl.ds(low, own_rows), :] for k in range(count)]
         return lax.dot_general(
             jnp.concatenate(left, axis=1), jnp.concatenate(right, axis=1), (((1,), (1,)), ((), ())),
             preferred_element_type=jnp.float32,
@@ -136,30 +137,25 @@
 
     def compute(piece):
         group = lax.div(piece, PIECES)
-        m = lax.rem(piece, PIECES // 2)
-
-        @pl.when(lax.rem(piece, PIECES) < PIECES // 2)
-        def _():
-            sums[m] = product(group, fetch_at, FETCH, m * 256, 256)
-
-        @pl.when(lax.rem(piece, PIECES) >= PIECES // 2)
-        def _():
-            add = icol[m]
-            total = sums[m] + product(group, other_at, OVER, m * 256, 256) + jnp.concatenate([add, add], axis=1)
-            best = jnp.max(total.reshape(2, 128, 8 * rows), axis=1)
-            part[2 * group, m] = best[:, 0:128]
-            part[2 * group + 1, m] = best[:, 128:256]
-
-    def finish():
-        sums[...] = product(3, fetch_at, FETCH, 0, 2 * own_rows).reshape(sums.shape)
-        x_arrived(3)
-        rest = product(3, other_at, OVER, 0, 2 * own_rows).reshape(sums.shape)
-        for m in range(4):
-            add = icol[m]
-            total = sums[m] + rest[m] + jnp.concatenate([add, add], axis=1)
-            best = jnp.max(total.reshape(2, 128, 8 * rows), axis=1)
-            part[6, m] = best[:, 0:128]
-            part[7, m] = best[:, 128:256]
+        which = lax.rem(piece, PIECES)
+        owner = lax.rem(core + which, 2)
+
+        @pl.when(which < 2)
+        def _():
+            sums[owner] = product(group, fetch_at, FETCH, owner)
+
+        @pl.when(which >= 2)
+        def _():
+            rest = product(group, other_at, OVER, owner)
+            lane = lax.broadcasted_iota(jnp.int32, (8 * rows, TILE), 1)
+            best = jnp.zeros((8 * rows, TILE), jnp.float32)
+            for n in range(4):
+                at = slice(n * 128, n * 128 + 128)
+                total = sums[owner, :, at] + rest[:, at] + offset[owner, n:n + 1, :]
+                best = jnp.where(lane == n, jnp.max(total, axis=1, keepdims=True), best)
+            turned = best.T
+            part[2 * group, owner] = turned[0:4, 0:128]
+            part[2 * group + 1, owner] = turned[0:4, 128:256]
 
     def tell(group):
         for i in range(max(8 * group, 1), 8 * group + 8):
@@ -173,10 +169,17 @@
     def column(k):
         return pl.ds(pl.multiple_of(k * TILE, TILE), TILE)
 
-    def own(k):
+    def own(k, sem):
         return pltpu.make_async_copy(
-            trial_ref.at[pl.ds(share * rows, rows), column(k)], gath.at[0, k], local_sem.at[0]
-        )
+            trial_ref.at[pl.ds(share * rows, rows), column(k)], gath.at[0, k], sem
+        )
+
+    own_parts = ((mine_at, OVER, local_sem.at[0]), (OVER, MIDDLE, local_sem.at[4]), (other_at, OVER, local_sem.at[5]))
+
+    def own_arrived(i):
+        at, count, sem = own_parts[i]
+        ref = gath.at[0, pl.ds(at, count)]
+        pltpu.make_async_copy(ref, ref, sem).wait()
 
     def load(k):
         return pltpu.make_async_copy(
@@ -200,25 +203,20 @@
         pl.semaphore_signal(barrier, inc=1, device_id=(node, beside[d]), device_id_type=MESH)
     for j in range(1, 8):
         pl.semaphore_signal(barrier, inc=1, device_id=((node + j) % 8, cut), device_id_type=MESH)
-    for k in range(tiles):
-        own(k).start()
+    for at, count, sem in own_parts:
+        for k in range(count):
+            own(at + k, sem).start()
     load_offset.start()
     load_trans.start()
     pl.semaphore_wait(barrier, 11)
-    pltpu.make_async_copy(gath.at[0], gath.at[0], local_sem.at[0]).wait()
-
-    for o, h, d in FIRST:
-        yz_copy(o, h, d).start()
+    for part_sent in PARTS:
+        own_arrived(part_sent)
+        for o, h, d in FIRST:
+            if h == part_sent:
+                yz_copy(o, h, d).start()
     swap_offset.start()
     for k in range(tiles):
         load(k).start()
-    load_offset.wait()
-    swap_offset.wait()
-    for c in range(2):
-        for n in range(4):
-            line = jnp.broadcast_to(offset[c, n:n + 1, :], (128, 128))
-            icol[2 * c + n // 2, pl.ds(n % 2 * 128, 128), :] = line.T
-
     pltpu.make_async_copy(loaded, loaded, local_sem.at[1]).wait()
     swap.start()
 
@@ -231,6 +229,10 @@
                 x_copy(o, 0).start()
                 x_copy(o, 1).start()
         if k == 0:
+            own_arrived(2)
+            load_offset.wait()
+        if k == 1:
+            swap_offset.wait()
             swap.wait()
         if k % PIECES == 0 and k > 0:
             tell(k // PIECES - 1)
@@ -257,8 +259,6 @@
         return carry
 
     lax.fori_loop(0, STEPS, turn, 0)
-    talk(STEPS)
-    finish()
     tell(3)
 
     for count, sem in ((FETCH, yz_send), (OVER, x_send)):
@@ -303,7 +303,7 @@
         pltpu.make_async_copy(ref, ref, b_send).wait()
 
     known = jnp.concatenate(
-        [nodev[2 * i + holder, m, :, 0:rows] for i in range(NX) for m in range(4)], axis=0
+        [nodev[2 * i + holder, m, :, 0:rows] for i in range(NX) for m in range(2)], axis=0
     )
     vals[...] = lax.dot_general(
         known.T, mixing, (((1,), (1,)), ((), ())),
@@ -329,13 +329,12 @@
             pltpu.VMEM((width // TILE, 2 * node_local * cut_local, TILE), jnp.bfloat16),
             pltpu.VMEM((2, node_local, cut_local), jnp.float32),
             pltpu.VMEM(transition.shape, jnp.float32),
-            pltpu.VMEM((4, 2 * cut_local, 128), jnp.float32),
-            pltpu.VMEM((4, 2 * cut_local, 4 * rows), jnp.float32),
-            pltpu.VMEM((count // 4, 4, 2, 128), jnp.float32),
-            pltpu.VMEM((count - 1, 4, 2, 128), jnp.float32),
-            pltpu.VMEM((8, 4, 2, 128), jnp.float32),
+            pltpu.VMEM((2, 4 * rows, node_local * cut_local), jnp.float32),
+            pltpu.VMEM((count // 4, 2, node_local, 128), jnp.float32),
+            pltpu.VMEM((count - 1, 2, node_local, 128), jnp.float32),
+            pltpu.VMEM((8, 2, node_local, 128), jnp.float32),
             pltpu.VMEM((rows // 2, nodes), jnp.float32),
-            sems((4,)),
+            sems((6,)),
             sems((2,)),
             sems((2,)),
             sems(()),

time: 56.9 us -> 56.9 us (level)
  no operation moved by 1% of the time
where the time goes in v3:
time: 56.9 us; the launch traced here: 56.7 us
  Pallas kernels  56.1 us (99%)
  local copies, waits for them, and re-layouts  0.6 us (1%)
    pallas_call x1, Pallas kernels, per_device(): pl.pallas_call(kernel, out_shape=jax.ShapeDtypeStruct((1, rows // 8, node...  56.1 us

profile of v3, /device:TPU:7, one launch (start us, length us, event | category | flops | bytes accessed | tf_op | source)
XLA Modules:
  0.0 56.7 jit_solution(5072462239392610091)
XLA Ops:
  0.0 56.1 %shard_map.46 = f32[1,8,32]{2,1,0:T(8,128)S(1)} custom-call(bf16[64,4096]{1,0:T(8,128)(2,1)} %trial_ref.1, bf16[512,4096]{1,0:T(8,128)(2,1)} %bitcast.1, f32[4,128]{1,0:T(4,128)} %offset_ref.1, f32[32,32]{1,0:T(8,128)} %trans_ref.1), custom_call_target="tpu_custom_call" | custom-call | flops 8589934592 | bytes 5242880 | tf_op jit(solution)/shard_map/pallas_call | solution.py:322
  56.1 0.6 %copy.6 = f32[1,8,32]{2,1,0:T(8,128)} copy(f32[1,8,32]{2,1,0:T(8,128)S(1)} %shard_map.46) | data formatting | bytes 2048

commit v4 on v3

--- a/solution.py
+++ b/solution.py
@@ -20,7 +20,7 @@
 CROSS = {
     PZ: [(0, 1), (0, 2), (0, 3), (2, 1), (0, 4), (2, 2), (2, 3), (1, 4)],
     MZ: [(0, -1), (0, -2), (0, -3), (2, -1), (2, -2), (2, -3), (2, 4)],
-    PY: [(1, 0), (2, 0), (1, 1), (1, -1), (1, 2), (1, -2), (1, 3), (1, -3)],
+    PY: [(1, 0), (2, 0), (1, 1), (1, -1), (1, 2), (1, 3), (1, -2), (1, -3)],
     MY: [(-1, 0), (-1, 1), (-1, -1), (-1, 2), (-1, -2), (-1, 3), (-1, -3), (-1, 4)],
 }
 PARTS = (0, 1)
@@ -31,7 +31,10 @@
 
 
 def plan(window, span, delay):
-    todo = {d: [(wrap(o), h) for o in order for h in PARTS] for d, order in CROSS.items()}
+    todo = {
+        d: [(wrap(o), h) for o in order[:-2] for h in PARTS] + [(wrap(o), h) for h in PARTS for o in order[-2:]]
+        for d, order in CROSS.items()
+    }
     here = {((0, 0), h) for h in PARTS}
     free = dict.fromkeys(LINKS, 0.0)
     flying = dict.fromkeys(LINKS, 0)
@@ -61,21 +64,23 @@
 
 
 FIRST, TURNS = plan(window=3, span=1.8, delay=2.5)
-PLACE = {(0, 0): 0}
-for o, h, _ in TURNS:
-    if (o, 1 - h) in [t[:2] for t in TURNS[:TURNS.index((o, h, _))]]:
-        PLACE[o] = len(PLACE)
-ARRIVALS = sorted(PLACE, key=PLACE.get)
-PIECES = 4
-NEED = [1 + max(i for i, t in enumerate(TURNS) if PLACE[t[0]] < 8 * g + 8) for g in range(4)]
+DONE = {o: i for i, (o, _, _) in enumerate(TURNS)}
+ARRIVALS = [(0, 0)] + sorted(DONE, key=DONE.get)
+PLACE = {o: i for i, o in enumerate(ARRIVALS)}
+PIECES = 6
 STEPS = 4 * PIECES
+LAST = 3 * PIECES
+NEED = [1 + max(i for i, t in enumerate(TURNS) if PLACE[t[0]] < 8 * g + 8) for g in range(3)]
+NEED.append(1 + max(i for i, t in enumerate(TURNS) if t[1] == 0))
 
 
 def handled(step):
-    group, which = step // PIECES, step % PIECES
     if step < 0:
         return 0
-    return NEED[group] + (NEED[min(group + 1, 3)] - NEED[group]) * which // PIECES
+    group, which = step // PIECES, step % PIECES
+    if group < 3:
+        return NEED[group] + (NEED[group + 1] - NEED[group]) * which // PIECES
+    return NEED[3] + (len(TURNS) - NEED[3]) * min(which, 4) // 4
 
 
 def kernel(
@@ -135,27 +140,31 @@
             preferred_element_type=jnp.float32,
         )
 
-    def compute(piece):
-        group = lax.div(piece, PIECES)
-        which = lax.rem(piece, PIECES)
+    def maximum(group, owner, rest):
+        lane = lax.broadcasted_iota(jnp.int32, (8 * rows, TILE), 1)
+        best = jnp.zeros((8 * rows, TILE), jnp.float32)
+        for n in range(4):
+            at = slice(n * 128, n * 128 + 128)
+            total = sums[owner, :, at] + rest[:, at] + offset[owner, n:n + 1, :]
+            best = jnp.where(lane == n, jnp.max(total, axis=1, keepdims=True), best)
+        turned = best.T
+        part[2 * group, owner] = turned[0:4, 0:128]
+        part[2 * group + 1, owner] = turned[0:4, 128:256]
+
+    def compute(group, which, ranges):
         owner = lax.rem(core + which, 2)
 
         @pl.when(which < 2)
         def _():
-            sums[owner] = product(group, fetch_at, FETCH, owner)
-
-        @pl.when(which >= 2)
-        def _():
-            rest = product(group, other_at, OVER, owner)
-            lane = lax.broadcasted_iota(jnp.int32, (8 * rows, TILE), 1)
-            best = jnp.zeros((8 * rows, TILE), jnp.float32)
-            for n in range(4):
-                at = slice(n * 128, n * 128 + 128)
-                total = sums[owner, :, at] + rest[:, at] + offset[owner, n:n + 1, :]
-                best = jnp.where(lane == n, jnp.max(total, axis=1, keepdims=True), best)
-            turned = best.T
-            part[2 * group, owner] = turned[0:4, 0:128]
-            part[2 * group + 1, owner] = turned[0:4, 128:256]
+            sums[owner] = product(group, *ranges[0], owner)
+
+        @pl.when(jnp.logical_and(which >= 2, which < 4))
+        def _():
+            sums[owner] = sums[owner] + product(group, *ranges[1], owner)
+
+        @pl.when(which >= 4)
+        def _():
+            maximum(group, owner, product(group, *ranges[2], owner))
 
     def tell(group):
         for i in range(max(8 * group, 1), 8 * group + 8):
@@ -236,7 +245,7 @@
             swap.wait()
         if k % PIECES == 0 and k > 0:
             tell(k // PIECES - 1)
-        if k % PIECES == PIECES // 2:
+        if k % PIECES == (2 if k >= LAST else 4):
             x_arrived(k // PIECES)
 
     def choose(step, low, high):
@@ -253,12 +262,20 @@
         def _():
             choose(step, mid, high)
 
+    over, middle, other = (mine_at, OVER), (OVER, MIDDLE), (other_at, OVER)
+
     def turn(step, carry):
-        choose(step, 0, STEPS)
-        compute(step)
+        choose(step, 0, LAST)
+        compute(lax.div(step, PIECES), lax.rem(step, PIECES), (over, middle, other))
         return carry
 
-    lax.fori_loop(0, STEPS, turn, 0)
+    def last_turn(step, carry):
+        choose(step, LAST, STEPS)
+        compute(3, lax.rem(step, PIECES), (over, other, middle))
+        return carry
+
+    lax.fori_loop(0, LAST, turn, 0)
+    lax.fori_loop(LAST, STEPS, last_turn, 0)
     tell(3)
 
     for count, sem in ((FETCH, yz_send), (OVER, x_send)):

time: 56.9 us -> 57.5 us (1.011)
  Pallas kernels: 56.1 us -> 56.8 us
    pallas_call x1, Pallas kernels: 56.1 us -> 56.8 us  [per_device(): pl.pallas_call(kernel, out_shape=jax.ShapeDtypeStruct((1, rows // 8, node...]
where the time goes in v4:
time: 57.5 us; the launch traced here: 57.4 us
  Pallas kernels  56.8 us (99%)
  local copies, waits for them, and re-layouts  0.6 us (1%)
    pallas_call x1, Pallas kernels, per_device(): pl.pallas_call(kernel, out_shape=jax.ShapeDtypeStruct((1, rows // 8, node...  56.8 us

profile of v4, /device:TPU:7, one launch (start us, length us, event | category | flops | bytes accessed | tf_op | source)
XLA Modules:
  0.0 57.4 jit_solution(1568724820299127953)
XLA Ops:
  0.0 56.8 %shard_map.46 = f32[1,8,32]{2,1,0:T(8,128)S(1)} custom-call(bf16[64,4096]{1,0:T(8,128)(2,1)} %trial_ref.1, bf16[512,4096]{1,0:T(8,128)(2,1)} %bitcast.1, f32[4,128]{1,0:T(4,128)} %offset_ref.1, f32[32,32]{1,0:T(8,128)} %trans_ref.1), custom_call_target="tpu_custom_call" | custom-call | flops 8589934592 | bytes 5242880 | tf_op jit(solution)/shard_map/pallas_call | solution.py:339
  56.8 0.6 %copy.6 = f32[1,8,32]{2,1,0:T(8,128)} copy(f32[1,8,32]{2,1,0:T(8,128)S(1)} %shard_map.46) | data formatting | bytes 2048

commit v5 on v3

--- a/solution.py
+++ b/solution.py
@@ -66,21 +66,25 @@
     if (o, 1 - h) in [t[:2] for t in TURNS[:TURNS.index((o, h, _))]]:
         PLACE[o] = len(PLACE)
 ARRIVALS = sorted(PLACE, key=PLACE.get)
-PIECES = 4
-NEED = [1 + max(i for i, t in enumerate(TURNS) if PLACE[t[0]] < 8 * g + 8) for g in range(4)]
-STEPS = 4 * PIECES
+GROUPS = ((0, 4), (4, 4), (8, 8), (16, 8), (24, 8))
+GROUP_OF = {first + i: g for g, (first, size) in enumerate(GROUPS) for i in range(size)}
+NEED = [1 + max(i for i, t in enumerate(TURNS) if PLACE[t[0]] < first + size) for first, size in GROUPS]
+SMALL, BOTH, LARGE, STEPS = 0, 4, 6, 18
+KNOTS = ((0, NEED[0]), (2, NEED[1]), (6, NEED[2]), (10, NEED[3]), (14, NEED[4]), (STEPS, NEED[4]))
+CROSSED = {1: 0, 3: 1, 8: 2, 12: 3, 16: 4}
+TOLD = {6: (0, 8), 10: (8, 8), 14: (16, 8)}
 
 
 def handled(step):
-    group, which = step // PIECES, step % PIECES
     if step < 0:
         return 0
-    return NEED[group] + (NEED[min(group + 1, 3)] - NEED[group]) * which // PIECES
+    low, high = [(p, q) for p, q in zip(KNOTS, KNOTS[1:]) if p[0] <= step < q[0]][0]
+    return low[1] + (high[1] - low[1]) * (step - low[0]) // (high[0] - low[0])
 
 
 def kernel(
     trial_ref, slope_ref, offset_ref, trans_ref, out_ref,
-    gath, slopes, offset, weights, sums, part, got, nodev, vals,
+    gath, slopes, offset, weights, mixing, sums, part, got, give, take,
     local_sem, swap_send, swap_recv, yz_send, yz_recv, x_send, x_recv, a_send, a_recv, b_send, b_recv,
 ):
     node = lax.axis_index("node")
@@ -117,48 +121,48 @@
         ref = gath.at[PLACE[o], pl.ds(mine_at + way * (OVER // 2), OVER // 2)]
         to = ((x + (1 if way == 0 else NX - 1)) % NX) * 2 + core
         return pltpu.make_async_remote_copy(
-            src_ref=ref, dst_ref=ref, send_sem=x_send, recv_sem=x_recv.at[PLACE[o] // 8],
+            src_ref=ref, dst_ref=ref, send_sem=x_send, recv_sem=x_recv.at[GROUP_OF[PLACE[o]]],
             device_id=(to, cut), device_id_type=MESH,
         )
 
     def x_arrived(group):
-        low = max(8 * group, 1)
-        ref = gath.at[pl.ds(low, 8 * group + 8 - low), pl.ds(other_at, OVER)]
+        first, size = GROUPS[group]
+        low = max(first, 1)
+        ref = gath.at[pl.ds(low, first + size - low), pl.ds(other_at, OVER)]
         pltpu.make_async_copy(ref, ref, x_recv.at[group]).wait()
 
-    def product(group, at, count, owner):
+    def product(first, size, at, count, owner):
         low = owner * own_rows
-        left = [gath[pl.ds(8 * group, 8), at + k].reshape(8 * rows, TILE) for k in range(count)]
+        left = [gath[pl.ds(first, size), at + k].reshape(size * rows, TILE) for k in range(count)]
         right = [slopes[at + k, pl.ds(low, own_rows), :] for k in range(count)]
         return lax.dot_general(
             jnp.concatenate(left, axis=1), jnp.concatenate(right, axis=1), (((1,), (1,)), ((), ())),
             preferred_element_type=jnp.float32,
         )
 
-    def compute(piece):
-        group = lax.div(piece, PIECES)
-        which = lax.rem(piece, PIECES)
+    def compute(first, size, which):
         owner = lax.rem(core + which, 2)
+        count = size * rows
 
         @pl.when(which < 2)
         def _():
-            sums[owner] = product(group, fetch_at, FETCH, owner)
+            sums[owner, 0:count] = product(first, size, fetch_at, FETCH, owner)
 
         @pl.when(which >= 2)
         def _():
-            rest = product(group, other_at, OVER, owner)
-            lane = lax.broadcasted_iota(jnp.int32, (8 * rows, TILE), 1)
-            best = jnp.zeros((8 * rows, TILE), jnp.float32)
+            rest = product(first, size, other_at, OVER, owner)
+            lane = lax.broadcasted_iota(jnp.int32, (count, TILE), 1)
+            best = jnp.zeros((count, TILE), jnp.float32)
             for n in range(4):
                 at = slice(n * 128, n * 128 + 128)
-                total = sums[owner, :, at] + rest[:, at] + offset[owner, n:n + 1, :]
+                total = sums[owner, 0:count, at] + rest[:, at] + offset[owner, n:n + 1, :]
                 best = jnp.where(lane == n, jnp.max(total, axis=1, keepdims=True), best)
             turned = best.T
-            part[2 * group, owner] = turned[0:4, 0:128]
-            part[2 * group + 1, owner] = turned[0:4, 128:256]
-
-    def tell(group):
-        for i in range(max(8 * group, 1), 8 * group + 8):
+            for j in range(size // 4):
+                part[first // 4 + j, owner] = turned[0:4, 128 * j:128 * j + 128]
+
+    def tell(first, size):
+        for i in range(max(first, 1), first + size):
             o = ARRIVALS[i]
             owner = ((y - o[0] + NY) % NY) * NZ + (z - o[1] + NZ) % NZ
             pltpu.make_async_remote_copy(
@@ -219,6 +223,9 @@
         load(k).start()
     pltpu.make_async_copy(loaded, loaded, local_sem.at[1]).wait()
     swap.start()
+    load_trans.wait()
+    trans = weights[...]
+    mixing[...] = (trans / jnp.sum(trans, axis=1, keepdims=True)).T
 
     def talk(k):
         for o, h, sends in TURNS[handled(k - 1):handled(k)]:
@@ -231,13 +238,13 @@
         if k == 0:
             own_arrived(2)
             load_offset.wait()
-        if k == 1:
+        if k == BOTH:
             swap_offset.wait()
             swap.wait()
-        if k % PIECES == 0 and k > 0:
-            tell(k // PIECES - 1)
-        if k % PIECES == PIECES // 2:
-            x_arrived(k // PIECES)
+        if k in TOLD:
+            tell(*TOLD[k])
+        if k in CROSSED:
+            x_arrived(CROSSED[k])
 
     def choose(step, low, high):
         if high - low == 1:
@@ -253,13 +260,21 @@
         def _():
             choose(step, mid, high)
 
+    def small_turn(step, carry):
+        choose(step, SMALL, BOTH)
+        compute(4 * lax.div(step, 2), 4, 2 * lax.rem(step, 2))
+        return carry
+
     def turn(step, carry):
-        choose(step, 0, STEPS)
-        compute(step)
+        choose(step, BOTH, STEPS)
+        both = step < LARGE
+        first = jnp.where(both, 0, 8 + 8 * lax.div(step - LARGE, 4))
+        compute(first, 8, jnp.where(both, 2 * (step - BOTH) + 1, lax.rem(step - LARGE, 4)))
         return carry
 
-    lax.fori_loop(0, STEPS, turn, 0)
-    tell(3)
+    lax.fori_loop(SMALL, BOTH, small_turn, 0)
+    lax.fori_loop(BOTH, STEPS, turn, 0)
+    tell(24, 8)
 
     for count, sem in ((FETCH, yz_send), (OVER, x_send)):
         ref = gath.at[pl.ds(0, len(ARRIVALS) - 1), pl.ds(0, count)]
@@ -273,43 +288,39 @@
             tiles.append(part[0])
         top = functools.reduce(jnp.maximum, tiles)[:, :, q * rows:(q + 1) * rows]
         best = top if best is None else jnp.maximum(best, top)
-    nodev[node, :, :, 0:rows] = best
+    states_down = jnp.concatenate([best[0], best[1]], axis=0).T
+    shares = mixing[pl.ds(pl.multiple_of(x * 8, 8), 8), :]
+    values = sum(states_down[:, i:i + 1] * shares[i:i + 1, :] for i in range(8))
+    for j in range(4):
+        give[j, :, 0:shares.shape[1]] = values[8 * j:8 * j + 8]
     for j in range(4):
         to = 4 * share + j
 
         @pl.when(to != node)
         def _():
             pltpu.make_async_remote_copy(
-                src_ref=nodev.at[node], dst_ref=nodev.at[node], send_sem=b_send, recv_sem=b_recv,
+                src_ref=give.at[j], dst_ref=take.at[x], send_sem=b_send, recv_sem=b_recv,
                 device_id=(to, cut), device_id_type=MESH,
             ).start()
 
-    load_trans.wait()
-    trans = weights[...]
-    mixing = trans / jnp.sum(trans, axis=1, keepdims=True)
-    holder = 1 - node // 4
-    keeps = holder == core
+        @pl.when(to == node)
+        def _():
+            take[x] = give[j]
+
+    keeps = 1 - node // 4 == core
 
     @pl.when(keeps)
     def _():
-        ref = nodev.at[pl.ds(0, 3)]
+        ref = take.at[pl.ds(0, 3)]
         pltpu.make_async_copy(ref, ref, b_recv).wait()
         pltpu.make_async_copy(ref, ref, b_send).wait()
 
     @pl.when(jnp.logical_not(keeps))
     def _():
-        ref = nodev.at[pl.ds(0, 4)]
-        pltpu.make_async_copy(ref, ref, b_recv).wait()
-        pltpu.make_async_copy(ref, ref, b_send).wait()
-
-    known = jnp.concatenate(
-        [nodev[2 * i + holder, m, :, 0:rows] for i in range(NX) for m in range(2)], axis=0
-    )
-    vals[...] = lax.dot_general(
-        known.T, mixing, (((1,), (1,)), ((), ())),
-        precision=lax.Precision.HIGHEST, preferred_element_type=jnp.float32,
-    )
-    out_ref[0] = vals[pl.ds(pl.multiple_of((node % 4) * 8, 8), 8), :]
+        pltpu.make_async_copy(take, take, b_recv).wait()
+        pltpu.make_async_copy(take, take, b_send).wait()
+
+    out_ref[0] = sum(take[i, :, 0:shares.shape[1]] for i in range(NX))
 
 
 def per_device(trial_states, cut_slopes, cut_intercepts, transition):
@@ -329,18 +340,19 @@
             pltpu.VMEM((width // TILE, 2 * node_local * cut_local, TILE), jnp.bfloat16),
             pltpu.VMEM((2, node_local, cut_local), jnp.float32),
             pltpu.VMEM(transition.shape, jnp.float32),
+            pltpu.VMEM(transition.shape, jnp.float32),
             pltpu.VMEM((2, 4 * rows, node_local * cut_local), jnp.float32),
             pltpu.VMEM((count // 4, 2, node_local, 128), jnp.float32),
             pltpu.VMEM((count - 1, 2, node_local, 128), jnp.float32),
-            pltpu.VMEM((8, 2, node_local, 128), jnp.float32),
-            pltpu.VMEM((rows // 2, nodes), jnp.float32),
+            pltpu.VMEM((4, 8, 128), jnp.float32),
+            pltpu.VMEM((4, 8, 128), jnp.float32),
             sems((6,)),
             sems((2,)),
             sems((2,)),
             sems(()),
             sems((count - 1, 2)),
             sems(()),
-            sems((count // 8,)),
+            sems((len(GROUPS),)),
             sems(()),
             sems(()),
             sems(()),

time: 56.9 us -> 57.7 us (1.014)
  Pallas kernels: 56.1 us -> 57 us
    pallas_call x1, Pallas kernels: 56.1 us -> 57 us  [per_device(): pl.pallas_call(kernel, out_shape=jax.ShapeDtypeStruct((1, rows // 8, node...]
where the time goes in v5:
time: 57.7 us; the launch traced here: 57.6 us
  Pallas kernels  57 us (99%)
  local copies, waits for them, and re-layouts  0.6 us (1%)
    pallas_call x1, Pallas kernels, per_device(): pl.pallas_call(kernel, out_shape=jax.ShapeDtypeStruct((1, rows // 8, node...  57 us

profile of v5, /device:TPU:7, one launch (start us, length us, event | category | flops | bytes accessed | tf_op | source)
XLA Modules:
  0.0 57.6 jit_solution(12472499729510080327)
XLA Ops:
  0.0 57.0 %shard_map.46 = f32[1,8,32]{2,1,0:T(8,128)S(1)} custom-call(bf16[64,4096]{1,0:T(8,128)(2,1)} %trial_ref.1, bf16[512,4096]{1,0:T(8,128)(2,1)} %bitcast.1, f32[4,128]{1,0:T(4,128)} %offset_ref.1, f32[32,32]{1,0:T(8,128)} %trans_ref.1), custom_call_target="tpu_custom_call" | custom-call | flops 8589934592 | bytes 5242880 | tf_op jit(solution)/shard_map/pallas_call | solution.py:333
  57.0 0.6 %copy.6 = f32[1,8,32]{2,1,0:T(8,128)} copy(f32[1,8,32]{2,1,0:T(8,128)S(1)} %shard_map.46) | data formatting | bytes 2048

commit v6 on v3

--- a/solution.py
+++ b/solution.py
@@ -23,15 +23,31 @@
     PY: [(1, 0), (2, 0), (1, 1), (1, -1), (1, 2), (1, -2), (1, 3), (1, -3)],
     MY: [(-1, 0), (-1, 1), (-1, -1), (-1, 2), (-1, -2), (-1, 3), (-1, -3), (-1, 4)],
 }
-PARTS = (0, 1)
+PARTS = (0, 1, 2, 3)
+OVER_PARTS = (0, 1)
+SPANS = ((0, 5), (5, 5), (OVER, 6), (OVER + 6, 6))
+TREES = (((1, 1), False), ((1, -1), False), ((1, 1), True), ((-1, 1), True))
 
 
 def wrap(o):
     return (o[0] % NY, o[1] % NZ)
 
 
+def arrival_links():
+    links = {}
+    for p, ((sy, sz), moved) in enumerate(TREES):
+        for d, order in CROSS.items():
+            for turn, o in enumerate(order):
+                d_here, turn_here = d, turn
+                if moved and o == (-1, 4):
+                    d_here, turn_here = MZ, len(order)
+                links[wrap((sy * o[0], sz * o[1])), p] = (sy * d_here[0], sz * d_here[1]), turn_here
+    return links
+
+
 def plan(window, span, delay):
-    todo = {d: [(wrap(o), h) for o in order for h in PARTS] for d, order in CROSS.items()}
+    links = arrival_links()
+    todo = {d: sorted((k for k in links if links[k][0] == d), key=lambda k: (links[k][1], k[1])) for d in LINKS}
     here = {((0, 0), h) for h in PARTS}
     free = dict.fromkeys(LINKS, 0.0)
     flying = dict.fromkeys(LINKS, 0)
@@ -60,12 +76,10 @@
     return first, turns
 
 
-FIRST, TURNS = plan(window=3, span=1.8, delay=2.5)
-PLACE = {(0, 0): 0}
-for o, h, _ in TURNS:
-    if (o, 1 - h) in [t[:2] for t in TURNS[:TURNS.index((o, h, _))]]:
-        PLACE[o] = len(PLACE)
-ARRIVALS = sorted(PLACE, key=PLACE.get)
+FIRST, TURNS = plan(window=6, span=1.1, delay=2.0)
+DONE = {o: i for i, (o, _, _) in enumerate(TURNS)}
+ARRIVALS = [(0, 0)] + sorted(DONE, key=DONE.get)
+PLACE = {o: i for i, o in enumerate(ARRIVALS)}
 PIECES = 4
 NEED = [1 + max(i for i, t in enumerate(TURNS) if PLACE[t[0]] < 8 * g + 8) for g in range(4)]
 STEPS = 4 * PIECES
@@ -99,7 +113,8 @@
     beside = {d: ((y + d[0] + NY) % NY) * NZ + (z + d[1] + NZ) % NZ for d in LINKS}
 
     def part_of(o, h):
-        return gath.at[PLACE[o], pl.ds(mine_at, OVER) if h == 0 else pl.ds(OVER, MIDDLE)]
+        at, count = SPANS[h]
+        return gath.at[PLACE[o], pl.ds(at + mine_at if h in OVER_PARTS else at, count)]
 
     def yz_copy(o, h, d):
         oc = wrap((o[0] + d[0], o[1] + d[1]))
@@ -113,9 +128,9 @@
         ref = part_of(o, h)
         pltpu.make_async_copy(ref, ref, yz_recv.at[PLACE[o] - 1, h]).wait()
 
-    def x_copy(o, way):
-        ref = gath.at[PLACE[o], pl.ds(mine_at + way * (OVER // 2), OVER // 2)]
-        to = ((x + (1 if way == 0 else NX - 1)) % NX) * 2 + core
+    def x_copy(o, h):
+        ref = part_of(o, h)
+        to = ((x + (1 if (PLACE[o] + h) % 2 else NX - 1)) % NX) * 2 + core
         return pltpu.make_async_remote_copy(
             src_ref=ref, dst_ref=ref, send_sem=x_send, recv_sem=x_recv.at[PLACE[o] // 8],
             device_id=(to, cut), device_id_type=MESH,
@@ -209,11 +224,14 @@
     load_offset.start()
     load_trans.start()
     pl.semaphore_wait(barrier, 11)
-    for part_sent in PARTS:
-        own_arrived(part_sent)
-        for o, h, d in FIRST:
-            if h == part_sent:
-                yz_copy(o, h, d).start()
+    own_arrived(0)
+    for o, h, d in FIRST:
+        if h in OVER_PARTS:
+            yz_copy(o, h, d).start()
+    own_arrived(1)
+    for o, h, d in FIRST:
+        if h not in OVER_PARTS:
+            yz_copy(o, h, d).start()
     swap_offset.start()
     for k in range(tiles):
         load(k).start()
@@ -225,9 +243,8 @@
             yz_arrived(o, h)
             for send in sends:
                 yz_copy(*send).start()
-            if h == 0:
-                x_copy(o, 0).start()
-                x_copy(o, 1).start()
+            if h in OVER_PARTS:
+                x_copy(o, h).start()
         if k == 0:
             own_arrived(2)
             load_offset.wait()
@@ -338,7 +355,7 @@
             sems((2,)),
             sems((2,)),
             sems(()),
-            sems((count - 1, 2)),
+            sems((count - 1, len(PARTS))),
             sems(()),
             sems((count // 8,)),
             sems(()),

time: 56.9 us -> 56.8 us (level)
  no operation moved by 1% of the time
where the time goes in v6:
time: 56.8 us; the launch traced here: 56.7 us
  Pallas kernels  56.1 us (99%)
  local copies, waits for them, and re-layouts  0.6 us (1%)
    pallas_call x1, Pallas kernels, per_device(): pl.pallas_call(kernel, out_shape=jax.ShapeDtypeStruct((1, rows // 8, node...  56.1 us

profile of v6, /device:TPU:7, one launch (start us, length us, event | category | flops | bytes accessed | tf_op | source)
XLA Modules:
  0.0 56.7 jit_solution(986771276453261264)
XLA Ops:
  0.0 56.1 %shard_map.46 = f32[1,8,32]{2,1,0:T(8,128)S(1)} custom-call(bf16[64,4096]{1,0:T(8,128)(2,1)} %trial_ref.1, bf16[512,4096]{1,0:T(8,128)(2,1)} %bitcast.1, f32[4,128]{1,0:T(4,128)} %offset_ref.1, f32[32,32]{1,0:T(8,128)} %trans_ref.1), custom_call_target="tpu_custom_call" | custom-call | flops 8589934592 | bytes 5242880 | tf_op jit(solution)/shard_map/pallas_call | solution.py:339
  56.1 0.6 %copy.6 = f32[1,8,32]{2,1,0:T(8,128)} copy(f32[1,8,32]{2,1,0:T(8,128)S(1)} %shard_map.46) | data formatting | bytes 2048

commit v7 on v6

--- a/solution.py
+++ b/solution.py
@@ -11,7 +11,7 @@
 
 NY, NZ, NX = 4, 8, 4
 
-TILE, OVER, MIDDLE = 128, 10, 12
+TILE, OVER, MIDDLE = 128, 11, 10
 FETCH = OVER + MIDDLE
 
 PZ, MZ, PY, MY = (0, 1), (0, -1), (1, 0), (-1, 0)
@@ -25,7 +25,7 @@
 }
 PARTS = (0, 1, 2, 3)
 OVER_PARTS = (0, 1)
-SPANS = ((0, 5), (5, 5), (OVER, 6), (OVER + 6, 6))
+SPANS = ((0, 6), (6, 5), (OVER, 5), (OVER + 5, 5))
 TREES = (((1, 1), False), ((1, -1), False), ((1, 1), True), ((-1, 1), True))
 
 

time: 56.8 us -> 56.5 us (level)
  no operation moved by 1% of the time
where the time goes in v7:
time: 56.5 us; the launch traced here: 56.3 us
  Pallas kernels  55.7 us (99%)
  local copies, waits for them, and re-layouts  0.6 us (1%)
    pallas_call x1, Pallas kernels, per_device(): pl.pallas_call(kernel, out_shape=jax.ShapeDtypeStruct((1, rows // 8, node...  55.7 us

profile of v7, /device:TPU:7, one launch (start us, length us, event | category | flops | bytes accessed | tf_op | source)
XLA Modules:
  0.0 56.3 jit_solution(11778811642253942141)
XLA Ops:
  0.0 55.7 %shard_map.46 = f32[1,8,32]{2,1,0:T(8,128)S(1)} custom-call(bf16[64,4096]{1,0:T(8,128)(2,1)} %trial_ref.1, bf16[512,4096]{1,0:T(8,128)(2,1)} %bitcast.1, f32[4,128]{1,0:T(4,128)} %offset_ref.1, f32[32,32]{1,0:T(8,128)} %trans_ref.1), custom_call_target="tpu_custom_call" | custom-call | flops 8589934592 | bytes 5242880 | tf_op jit(solution)/shard_map/pallas_call | solution.py:339
  55.7 0.6 %copy.6 = f32[1,8,32]{2,1,0:T(8,128)} copy(f32[1,8,32]{2,1,0:T(8,128)S(1)} %shard_map.46) | data formatting | bytes 2048

commit v8 on v7

--- a/solution.py
+++ b/solution.py
@@ -81,6 +81,7 @@
 ARRIVALS = [(0, 0)] + sorted(DONE, key=DONE.get)
 PLACE = {o: i for i, o in enumerate(ARRIVALS)}
 PIECES = 4
+PACE = (0, 4, 12, 14)
 NEED = [1 + max(i for i, t in enumerate(TURNS) if PLACE[t[0]] < 8 * g + 8) for g in range(4)]
 STEPS = 4 * PIECES
 
@@ -89,7 +90,7 @@
     group, which = step // PIECES, step % PIECES
     if step < 0:
         return 0
-    return NEED[group] + (NEED[min(group + 1, 3)] - NEED[group]) * which // PIECES
+    return NEED[group] + (NEED[min(group + 1, 3)] - NEED[group]) * PACE[which] // 16
 
 
 def kernel(

time: 56.5 us -> 56.4 us (level)
  no operation moved by 1% of the time
where the time goes in v8:
time: 56.4 us; the launch traced here: 56.3 us
  Pallas kernels  55.7 us (99%)
  local copies, waits for them, and re-layouts  0.6 us (1%)
    pallas_call x1, Pallas kernels, per_device(): pl.pallas_call(kernel, out_shape=jax.ShapeDtypeStruct((1, rows // 8, node...  55.7 us

profile of v8, /device:TPU:7, one launch (start us, length us, event | category | flops | bytes accessed | tf_op | source)
XLA Modules:
  0.0 56.3 jit_solution(8706551469925322639)
XLA Ops:
  0.0 55.7 %shard_map.46 = f32[1,8,32]{2,1,0:T(8,128)S(1)} custom-call(bf16[64,4096]{1,0:T(8,128)(2,1)} %trial_ref.1, bf16[512,4096]{1,0:T(8,128)(2,1)} %bitcast.1, f32[4,128]{1,0:T(4,128)} %offset_ref.1, f32[32,32]{1,0:T(8,128)} %trans_ref.1), custom_call_target="tpu_custom_call" | custom-call | flops 8589934592 | bytes 5242880 | tf_op jit(solution)/shard_map/pallas_call | solution.py:340
  55.7 0.6 %copy.6 = f32[1,8,32]{2,1,0:T(8,128)} copy(f32[1,8,32]{2,1,0:T(8,128)S(1)} %shard_map.46) | data formatting | bytes 2048

commit v9 on v8

--- a/solution.py
+++ b/solution.py
@@ -47,7 +47,12 @@
 
 def plan(window, span, delay):
     links = arrival_links()
-    todo = {d: sorted((k for k in links if links[k][0] == d), key=lambda k: (links[k][1], k[1])) for d in LINKS}
+    todo = {
+        d: sorted(
+            (k for k in links if links[k][0] == d), key=lambda k: (links[k][1] + (k[1] not in OVER_PARTS), k[1])
+        )
+        for d in LINKS
+    }
     here = {((0, 0), h) for h in PARTS}
     free = dict.fromkeys(LINKS, 0.0)
     flying = dict.fromkeys(LINKS, 0)

time: 56.4 us -> 58 us (1.028)
  Pallas kernels: 55.7 us -> 57.3 us
    pallas_call x1, Pallas kernels: 55.7 us -> 57.3 us  [per_device(): pl.pallas_call(kernel, out_shape=jax.ShapeDtypeStruct((1, rows // 8, node...]
where the time goes in v9:
time: 58 us; the launch traced here: 57.9 us
  Pallas kernels  57.3 us (99%)
  local copies, waits for them, and re-layouts  0.6 us (1%)
    pallas_call x1, Pallas kernels, per_device(): pl.pallas_call(kernel, out_shape=jax.ShapeDtypeStruct((1, rows // 8, node...  57.3 us

profile of v9, /device:TPU:7, one launch (start us, length us, event | category | flops | bytes accessed | tf_op | source)
XLA Modules:
  0.0 57.9 jit_solution(5112049781832573633)
XLA Ops:
  0.0 57.3 %shard_map.46 = f32[1,8,32]{2,1,0:T(8,128)S(1)} custom-call(bf16[64,4096]{1,0:T(8,128)(2,1)} %trial_ref.1, bf16[512,4096]{1,0:T(8,128)(2,1)} %bitcast.1, f32[4,128]{1,0:T(4,128)} %offset_ref.1, f32[32,32]{1,0:T(8,128)} %trans_ref.1), custom_call_target="tpu_custom_call" | custom-call | flops 8589934592 | bytes 5242880 | tf_op jit(solution)/shard_map/pallas_call | solution.py:345
  57.4 0.6 %copy.6 = f32[1,8,32]{2,1,0:T(8,128)} copy(f32[1,8,32]{2,1,0:T(8,128)S(1)} %shard_map.46) | data formatting | bytes 2048

commit v10 on v8

--- a/solution.py
+++ b/solution.py
@@ -26,7 +26,7 @@
 PARTS = (0, 1, 2, 3)
 OVER_PARTS = (0, 1)
 SPANS = ((0, 6), (6, 5), (OVER, 5), (OVER + 5, 5))
-TREES = (((1, 1), False), ((1, -1), False), ((1, 1), True), ((-1, 1), True))
+MOVED = ({}, {(0, 4): (MZ, 3.5)}, {(-1, 4): (MZ, 7)}, {(1, -3): (MZ, 7)})
 
 
 def wrap(o):
@@ -35,13 +35,10 @@
 
 def arrival_links():
     links = {}
-    for p, ((sy, sz), moved) in enumerate(TREES):
+    for p, moved in enumerate(MOVED):
         for d, order in CROSS.items():
             for turn, o in enumerate(order):
-                d_here, turn_here = d, turn
-                if moved and o == (-1, 4):
-                    d_here, turn_here = MZ, len(order)
-                links[wrap((sy * o[0], sz * o[1])), p] = (sy * d_here[0], sz * d_here[1]), turn_here
+                links[wrap(o), p] = moved.get(o, (d, turn))
     return links
 
 

time: 56.4 us -> 56.5 us (level)
  no operation moved by 1% of the time
where the time goes in v10:
time: 56.5 us; the launch traced here: 56.4 us
  Pallas kernels  55.8 us (99%)
  local copies, waits for them, and re-layouts  0.6 us (1%)
    pallas_call x1, Pallas kernels, per_device(): pl.pallas_call(kernel, out_shape=jax.ShapeDtypeStruct((1, rows // 8, node...  55.8 us

profile of v10, /device:TPU:7, one launch (start us, length us, event | category | flops | bytes accessed | tf_op | source)
XLA Modules:
  0.0 56.4 jit_solution(5954056680008555402)
XLA Ops:
  0.0 55.8 %shard_map.46 = f32[1,8,32]{2,1,0:T(8,128)S(1)} custom-call(bf16[64,4096]{1,0:T(8,128)(2,1)} %trial_ref.1, bf16[512,4096]{1,0:T(8,128)(2,1)} %bitcast.1, f32[4,128]{1,0:T(4,128)} %offset_ref.1, f32[32,32]{1,0:T(8,128)} %trans_ref.1), custom_call_target="tpu_custom_call" | custom-call | flops 8589934592 | bytes 5242880 | tf_op jit(solution)/shard_map/pallas_call | solution.py:337
  55.8 0.6 %copy.6 = f32[1,8,32]{2,1,0:T(8,128)} copy(f32[1,8,32]{2,1,0:T(8,128)S(1)} %shard_map.46) | data formatting | bytes 2048

commit v11 on v8

--- a/solution.py
+++ b/solution.py
@@ -76,7 +76,7 @@
     return first, turns
 
 
-FIRST, TURNS = plan(window=6, span=1.1, delay=2.0)
+FIRST, TURNS = plan(window=4, span=1.1, delay=2.0)
 DONE = {o: i for i, (o, _, _) in enumerate(TURNS)}
 ARRIVALS = [(0, 0)] + sorted(DONE, key=DONE.get)
 PLACE = {o: i for i, o in enumerate(ARRIVALS)}

time: 56.4 us -> 58.5 us (1.037)
  Pallas kernels: 55.7 us -> 57.9 us
    pallas_call x1, Pallas kernels: 55.7 us -> 57.9 us  [per_device(): pl.pallas_call(kernel, out_shape=jax.ShapeDtypeStruct((1, rows // 8, node...]
where the time goes in v11:
time: 58.5 us
  Pallas kernels  57.9 us (99%)
  local copies, waits for them, and re-layouts  0.6 us (1%)
    pallas_call x1, Pallas kernels, per_device(): pl.pallas_call(kernel, out_shape=jax.ShapeDtypeStruct((1, rows // 8, node...  57.9 us

profile of v11, /device:TPU:7, one launch (start us, length us, event | category | flops | bytes accessed | tf_op | source)
XLA Modules:
  0.0 58.5 jit_solution(9421754685883934383)
XLA Ops:
  0.0 57.9 %shard_map.46 = f32[1,8,32]{2,1,0:T(8,128)S(1)} custom-call(bf16[64,4096]{1,0:T(8,128)(2,1)} %trial_ref.1, bf16[512,4096]{1,0:T(8,128)(2,1)} %bitcast.1, f32[4,128]{1,0:T(4,128)} %offset_ref.1, f32[32,32]{1,0:T(8,128)} %trans_ref.1), custom_call_target="tpu_custom_call" | custom-call | flops 8589934592 | bytes 5242880 | tf_op jit(solution)/shard_map/pallas_call | solution.py:340
  57.9 0.6 %copy.6 = f32[1,8,32]{2,1,0:T(8,128)} copy(f32[1,8,32]{2,1,0:T(8,128)S(1)} %shard_map.46) | data formatting | bytes 2048
